TPU v7x, 256 devices: a whole 4x4x8 slice. The times are simulated.
256 devices in a mesh: head: 4 (over x_lo, core), seq: 64 (over z, y, x_hi).
Axes of the slice: x: 4 (x_hi: 2, x_lo: 2; x = x_hi * 2 + x_lo), y: 4, z: 8, core: 2. Of those that a mesh axis runs over, the one named last changes fastest.
Arguments:
- query: float32 [32768, 2048], P(('seq', 'head')), may hold values from -8 to 8
- key_in: float32 [32768, 1024], P(('seq', 'head')), may hold values from -8 to 8
- value_in: float32 [32768, 1024], P(('seq', 'head')), may hold values from -6 to 6
- d_out: float32 [32768, 2048], P(('seq', 'head')), may hold values from -48 to 48
Outputs:
- grad_query: float32 [32768, 2048], P(('seq', 'head'))
- grad_key: float32 [32768, 1024], P(('seq', 'head'))
- grad_value: float32 [32768, 1024], P(('seq', 'head'))
All inputs are finite; a program needn't handle non-finite values.
Results may differ from a plain program's by a relative error of at most 0.00045.
Values sent between devices are 32-bit elements; how exact they have to be, the bound alone decides.
A program may use at most 64 MiB of HBM per device.

v0:
```python
import jax
import jax.numpy as jnp
from jax import lax
from jax.sharding import PartitionSpec as P

HD = 128
WINDOW = 1024


score_scale = 168.0 ** (-0.5)
highest = lax.Precision.HIGHEST


def shifted(value, axis, by):
    devices = lax.axis_size(axis)
    pairs = [(i, i + by) for i in range(devices) if 0 <= i + by < devices]
    return lax.ppermute(value, axis, pairs)


def side_by_side(arrays, axis, split_dim, concat_dim, along):
    widths = [a.shape[along] for a in arrays]
    both = jnp.concatenate(arrays, axis=along)
    whole = lax.all_to_all(both, axis, split_axis=split_dim, concat_axis=concat_dim, tiled=True)
    return tuple(jnp.split(whole, [sum(widths[:k]) for k in range(1, len(widths))], axis=along))


def band_grads(query_block, key_block, value_block, grad_block, start, reach):
    shard_rows = query_block.shape[0]
    key_rows = key_block.shape[0]
    group_size = query_block.shape[1] // key_block.shape[1]
    query_heads = query_block.reshape(shard_rows, -1, group_size, HD)
    grad_heads = grad_block.reshape(shard_rows, -1, group_size, HD)
    key_heads = key_block.reshape(key_rows, -1, HD)
    value_heads = value_block.reshape(key_rows, -1, HD)
    scores = jnp.einsum("qkgd,pkd->kgqp", query_heads, key_heads, precision=highest) * score_scale
    query_index = start + jnp.arange(shard_rows, dtype=jnp.int32)[:, None]
    key_index = start - 2 * shard_rows + jnp.arange(key_rows, dtype=jnp.int32)[None, :]
    inside = (key_index <= query_index) & (key_index > query_index - reach) & (key_index >= 0)
    scores = jnp.where(inside, scores, -jnp.inf)
    highest_score = jnp.max(scores, axis=-1, keepdims=True)
    raised = jnp.exp(scores - highest_score)
    weights = raised / jnp.sum(raised, axis=-1, keepdims=True)
    output = jnp.einsum("kgqp,pkd->qkgd", weights, value_heads, precision=highest)
    row_dot = jnp.einsum("qkgd,qkgd->kgq", grad_heads, output, precision=highest)
    grad_weight = jnp.einsum("qkgd,pkd->kgqp", grad_heads, value_heads, precision=highest)
    grad_score = weights * (grad_weight - row_dot[..., None])
    grad_query = (
        jnp.einsum("kgqp,pkd->qkgd", grad_score, key_heads, precision=highest) * score_scale
    )
    grad_key = (
        jnp.einsum("kgqp,qkgd->pkd", grad_score, query_heads, precision=highest) * score_scale
    )
    grad_value = jnp.einsum("kgqp,qkgd->pkd", weights, grad_heads, precision=highest)
    return (
        grad_query.reshape(shard_rows, -1),
        grad_key.reshape(key_rows, -1),
        grad_value.reshape(key_rows, -1),
    )


def heads_work(pieces):
    query4, key4, value4, grad4 = pieces
    shard_rows = query4.shape[0]
    kv_count = query4.shape[2]
    group_cols = query4.shape[3]
    query = query4.reshape(shard_rows, kv_count * group_cols)
    d_out = grad4.reshape(shard_rows, kv_count * group_cols)
    key_in = key4.reshape(shard_rows, kv_count * HD)
    value_in = value4.reshape(shard_rows, kv_count * HD)
    start = lax.axis_index("seq") * shard_rows
    nearby = shifted((key_in, value_in), "seq", 1)
    distant = shifted((nearby[0], nearby[1]), "seq", 1)
    all_keys = jnp.concatenate([distant[0], nearby[0], key_in], axis=0)
    all_values = jnp.concatenate([distant[1], nearby[1], value_in], axis=0)
    query_parts = []
    key_parts = []
    value_parts = []
    for column in range(kv_count):
        query_cols = slice(column * group_cols, (column + 1) * group_cols)
        kv_cols = slice(column * HD, (column + 1) * HD)
        grad_query, grad_key, grad_value = band_grads(
            query[:, query_cols],
            all_keys[:, kv_cols],
            all_values[:, kv_cols],
            d_out[:, query_cols],
            start,
            WINDOW,
        )
        query_parts.append(grad_query)
        key_parts.append(grad_key)
        value_parts.append(grad_value)
    grad_query = jnp.concatenate(query_parts, axis=1)
    grad_key = jnp.concatenate(key_parts, axis=1)
    grad_value = jnp.concatenate(value_parts, axis=1)
    far_part = (grad_key[:shard_rows], grad_value[:shard_rows])
    near_part = (grad_key[shard_rows : 2 * shard_rows], grad_value[shard_rows : 2 * shard_rows])
    own_key = grad_key[2 * shard_rows :]
    own_value = grad_value[2 * shard_rows :]
    passed = shifted((far_part[0], far_part[1]), "seq", -1)
    summed = (near_part[0] + passed[0], near_part[1] + passed[1])
    arrived = shifted((summed[0], summed[1]), "seq", -1)
    total_key = own_key + arrived[0]
    total_value = own_value + arrived[1]
    return (
        grad_query.reshape(shard_rows, 1, kv_count, group_cols),
        total_key.reshape(shard_rows, 1, kv_count, HD),
        total_value.reshape(shard_rows, 1, kv_count, HD),
    )


def per_device(query, key_in, value_in, d_out):
    head_count = lax.axis_size("head")
    local_rows = query.shape[0]
    kv_local = key_in.shape[1] // HD // head_count
    group_cols = query.shape[1] // (key_in.shape[1] // HD)
    query4 = query.reshape(local_rows, head_count, kv_local, group_cols)
    grad4 = d_out.reshape(local_rows, head_count, kv_local, group_cols)
    key4 = key_in.reshape(local_rows, head_count, kv_local, HD)
    value4 = value_in.reshape(local_rows, head_count, kv_local, HD)
    moved = side_by_side((query4, key4, value4, grad4), "head", 1, 0, 3)
    results = heads_work(moved)
    back = side_by_side((results[0], results[1], results[2]), "head", 0, 1, 3)
    return (
        back[0].reshape(local_rows, -1),
        back[1].reshape(local_rows, -1),
        back[2].reshape(local_rows, -1),
    )


def solution(mesh):
    return jax.shard_map(
        per_device,
        mesh=mesh,
        in_specs=(
            P(("seq", "head"), None),
            P(("seq", "head"), None),
            P(("seq", "head"), None),
            P(("seq", "head"), None),
        ),
        out_specs=(P(("seq", "head"), None), P(("seq", "head"), None), P(("seq", "head"), None)),
        check_vma=False,
    )
```

profile of v0, /device:TPU:127, one launch (start us, length us, event | category | flops | bytes accessed | tf_op | source)
XLA Modules:
  0.0 252.2 jit_solution(2110461224031348533)
XLA Ops:
  11.8 3.5 %copy.101 = f32[128,4,2,768]{3,2,0,1:T(2,128)} copy(f32[128,4,2,768]{0,3,2,1:T(8,128)S(1)} %pad_maximum_fusion) | data formatting | bytes 6291456 | tf_op jit(solution)/shard_map/concatenate | solution.py:22
  15.4 4.8 %all-to-all-start = ((f32[128,4,2,768]{3,2,0,1:T(2,128)}), f32[128,4,2,768]{3,2,0,1:T(2,128)S(1)}, u32[]{:S(2)}, u32[]{:S(2)}) async-start(f32[128,4,2,768]{3,2,0,1:T(2,128)} %copy.101), calls=%async_computation | async-start | bytes 6291456 | tf_op jit(solution)/shard_map/all_to_all | solution.py:23
  20.2 35.0 %all-to-all-done = f32[128,4,2,768]{3,2,0,1:T(2,128)S(1)} async-done(((f32[128,4,2,768]{3,2,0,1:T(2,128)}), f32[128,4,2,768]{3,2,0,1:T(2,128)S(1)}, u32[]{:S(2)}, u32[]{:S(2)}) %all-to-all-start) | async-done | bytes 3145760 | tf_op jit(solution)/shard_map/all_to_all | solution.py:23
  58.0 5.0 %collective-permute-start = (f32[512,256]{1,0:T(8,128)}, f32[512,256]{1,0:T(8,128)}, u32[]{:S(2)}, u32[]{:S(2)}) collective-permute-start(f32[512,256]{1,0:T(8,128)} %bitcast.247), channel_id=1, source_target_pairs={{0,1},{1,2},{2,3},{3,4},{4,5},{5,6},{6,7},{7,8},{8,9},{9,10},{10,1... | collective-permute-start | bytes 1572872 | tf_op jit(solution)/shard_map/ppermute | solution.py:17
  71.0 4.0 %collective-permute-start.2 = (f32[512,256]{1,0:T(8,128)S(1)}, f32[512,256]{1,0:T(8,128)S(1)}, u32[]{:S(2)}, u32[]{:S(2)}) collective-permute-start(f32[512,256]{1,0:T(8,128)S(1)} %bitcast.274), channel_id=1, source_target_pairs={{0,1},{1,2},{2,3},{3,4},{4,5},{5,6},{6,7},{7,8},{8,9},{9,10},{10,1... | collective-permute-start | bytes 1572872 | tf_op jit(solution)/shard_map/ppermute | solution.py:17
  75.1 8.7 %collective-permute-start.1 = (f32[512,256]{1,0:T(8,128)}, f32[512,256]{1,0:T(8,128)S(1)}, u32[]{:S(2)}, u32[]{:S(2)}) collective-permute-start(f32[512,256]{1,0:T(8,128)} %collective-permute-done), channel_id=1, source_target_pairs={{0,1},{1,2},{2,3},{3,4},{4,5},{5,6},{6,7},{7,8},{8,9},{9,10},{10,1... | collective-permute-start | bytes 1572872 | tf_op jit(solution)/shard_map/ppermute | solution.py:17
  87.0 8.4 %collective-permute-start.3 = (f32[512,256]{1,0:T(8,128)S(1)}, f32[512,256]{1,0:T(8,128)S(1)}, u32[]{:S(2)}, u32[]{:S(2)}) collective-permute-start(f32[512,256]{1,0:T(8,128)S(1)} %collective-permute-done.2), channel_id=1, source_target_pairs={{0,1},{1,2},{2,3},{3,4},{4,5},{5,6},{6,7},{7,8},{8,9},{9,10},{10,1... | collective-permute-start | bytes 1572872 | tf_op jit(solution)/shard_map/ppermute | solution.py:17
  99.4 6.0 %fusion.16 = (f32[2,512]{1,0:T(2,128)S(1)}, f32[1536,512,2]{1,0,2:T(8,128)S(1)}) fusion(pred[512,1536]{0,1:T(8,128)(4,1)S(1)} %copy-done, f32[512,2,128]{0,2,1:T(8,128)S(1)} %bitcast.256, f32[1536,256]{1,0:T(8,128)S(1)} %constant_dynamic-update-slice_fusion), kind=kOutput, calls=%fused_computation.22 | convolution fusion | flops 2420636672 | bytes 8392704 | tf_op jit(solution)/shard_map/qkgd,pkd->kgqp/dot_general | solution.py:35
  105.4 7.9 %fusion.13 = (f32[2,512]{1,0:T(2,128)S(1)}, f32[2,512]{1,0:T(2,128)S(1)}, f32[1536,512,2]{1,0,2:T(8,128)S(1)}) fusion(f32[1536,512,2]{1,0,2:T(8,128)S(1)} %get-tuple-element.25, f32[2,512]{1,0:T(2,128)S(1)} %get-tuple-element.24, pred[512,1536]{0,1:T(8,128)(4,1)S(1)} %copy-done, f32[512,2,128]{0,2,1:T(8,128)S(1)} %bitcast.270, ...), kind=kOutput, calls=%fused_computation.19 | convolution fusion | flops 2426927104 | bytes 14692352 | tf_op jit(solution)/shard_map/qkgd,pkd->kgqp/dot_general | solution.py:35
  114.8 7.7 %fusion.21 = f32[1536,128]{0,1:T(8,128)S(1)} fusion(f32[512,2,128]{0,2,1:T(8,128)S(1)} %bitcast.278, f32[1536,512,2]{1,0,2:T(8,128)S(1)} %get-tuple-element.26, f32[2,512]{1,0:T(2,128)S(1)} %fusion.15, f32[2,512]{1,0:T(2,128)S(1)} %get-tuple-element.13, pred[512,1536]{0,1:T(8,128)(4,1)S(1)} %copy-done), kind=kOutput, calls=%fused_computation.27 | convolution fusion | flops 2422210560 | bytes 8396800 | tf_op jit(solution)/shard_map/kgqp,qkgd->pkd/dot_general | solution.py:53
  122.5 7.8 %fusion.18 = f32[1536,128]{0,1:T(8,128)S(1)} fusion(f32[512,2,128]{0,2,1:T(8,128)S(1)} %bitcast.275, f32[1536,512,2]{1,0,2:T(8,128)S(1)} %get-tuple-element.25, f32[2,512]{1,0:T(2,128)S(1)} %get-tuple-element.12, f32[2,512]{1,0:T(2,128)S(1)} %get-tuple-element.24, pred[512,1536]{0,1:T(8,128)(4,1)S(1)} %copy-done), kind=kOutput, calls=%fused_computation.26 | convolution fusion | flops 2422210560 | bytes 8396800 | tf_op jit(solution)/shard_map/kgqp,qkgd->pkd/dot_general | solution.py:53
  133.2 5.4 %fusion.47 = f32[2,512]{1,0:T(2,128)S(1)} fusion(f32[2,512,128]{1,2,0:T(8,128)S(1)} %bitcast.279, f32[2,512]{1,0:T(2,128)S(1)} %fusion.15, f32[2,512]{1,0:T(2,128)S(1)} %get-tuple-element.13, f32[1536,512,2]{1,0,2:T(8,128)S(1)} %get-tuple-element.26, pred[512,1536]{0,1:T(8,128)(4,1)S(1)} %copy-done, f32[1536,256]{1,0:T(8,128)S(1)} %constant_dynamic-update-slice_fusion.3), kind=kOutput, calls=%fused_computation.50 | convolution fusion | flops 2422471680 | bytes 8400896 | tf_op jit(solution)/shard_map/kgqp,pkd->qkgd/dot_general | solution.py:43
  138.6 7.6 %fusion.1 = f32[2,512,1536]{1,2,0:T(8,128)S(1)} fusion(f32[512,2,128]{0,2,1:T(8,128)S(1)} %bitcast.280, f32[2,512]{1,0:T(2,128)S(1)} %fusion.47, f32[2,512]{1,0:T(2,128)S(1)} %fusion.15, f32[2,512]{1,0:T(2,128)S(1)} %get-tuple-element.13, f32[1536,512,2]{1,0,2:T(8,128)S(1)} %get-tuple-element.26, pred[512,1536]{0,1:T(8,128)(4,1)S(1)} %copy-done, ...), kind=kOutput, calls=%fused_computation.2 | convolution fusion | flops 2425356288 | bytes 14692352 | tf_op jit(solution)/shard_map/qkgd,pkd->kgqp/dot_general | solution.py:45
  146.2 6.5 %fusion.25 = f32[1536,128]{0,1:T(8,128)S(1)} fusion(f32[512,2,128]{0,2,1:T(8,128)S(1)} %bitcast.271, f32[2,512,1536]{1,2,0:T(8,128)S(1)} %fusion.1), kind=kOutput, calls=%fused_computation.30 | convolution fusion | flops 2416115712 | bytes 7602176 | tf_op jit(solution)/shard_map/kgqp,qkgd->pkd/dot_general | solution.py:51
  152.7 5.4 %fusion.44 = f32[2,512]{1,0:T(2,128)S(1)} fusion(f32[2,512,128]{1,2,0:T(8,128)S(1)} %bitcast.276, f32[2,512]{1,0:T(2,128)S(1)} %get-tuple-element.12, f32[2,512]{1,0:T(2,128)S(1)} %get-tuple-element.24, f32[1536,512,2]{1,0,2:T(8,128)S(1)} %get-tuple-element.25, pred[512,1536]{0,1:T(8,128)(4,1)S(1)} %copy-done, ...), kind=kOutput, calls=%fused_computation.49 | convolution fusion | flops 2422471680 | bytes 8400896 | tf_op jit(solution)/shard_map/kgqp,pkd->qkgd/dot_general | solution.py:43
  158.1 7.3 %fusion.3 = f32[2,512,1536]{1,2,0:T(8,128)S(1)} fusion(f32[512,2,128]{0,2,1:T(8,128)S(1)} %bitcast.277, f32[2,512]{1,0:T(2,128)S(1)} %fusion.44, f32[2,512]{1,0:T(2,128)S(1)} %get-tuple-element.12, f32[2,512]{1,0:T(2,128)S(1)} %get-tuple-element.24, f32[1536,512,2]{1,0,2:T(8,128)S(1)} %get-tuple-element.25, pred[512,1536]{0,1:T(8,128)(4,1)S(1)} %copy-done, ...), kind=kOutput, calls=%fused_computation.6 | convolution fusion | flops 2425356288 | bytes 14692352 | tf_op jit(solution)/shard_map/qkgd,pkd->kgqp/dot_general | solution.py:45
  165.5 6.5 %fusion.27 = f32[1536,128]{0,1:T(8,128)S(1)} fusion(f32[512,2,128]{0,2,1:T(8,128)S(1)} %bitcast.257, f32[2,512,1536]{1,2,0:T(8,128)S(1)} %fusion.3), kind=kOutput, calls=%fused_computation.33 | convolution fusion | flops 2416115712 | bytes 7602176 | tf_op jit(solution)/shard_map/kgqp,qkgd->pkd/dot_general | solution.py:51
  175.0 3.6 %convolution_multiply_fusion = f32[128,2,512]{2,0,1:T(8,128)S(1)} fusion(f32[2,512,1536]{1,2,0:T(8,128)S(1)} %fusion.1, f32[1536,256]{1,0:T(8,128)S(1)} %constant_dynamic-update-slice_fusion), kind=kOutput, calls=%fused_computation.43 | convolution fusion | flops 2416050176 | bytes 7602176 | tf_op jit(solution)/shard_map/kgqp,pkd->qkgd/dot_general | solution.py:48
  178.8 4.2 %collective-permute-start.7 = (f32[512,256]{0,1:T(8,128)S(1)}, f32[512,256]{0,1:T(8,128)S(1)}, u32[]{:S(2)}, u32[]{:S(2)}) collective-permute-start(f32[512,256]{0,1:T(8,128)S(1)} %fusion.53), channel_id=1, source_target_pairs={{1,0},{2,1},{3,2},{4,3},{5,4},{6,5},{7,6},{8,7},{9,8},{10,9},{11,1... | collective-permute-start | bytes 1572872 | tf_op jit(solution)/shard_map/ppermute | solution.py:17
  183.0 6.7 %collective-permute-done.4 = f32[512,256]{0,1:T(8,128)S(1)} collective-permute-done((f32[512,256]{0,1:T(8,128)S(1)}, f32[512,256]{0,1:T(8,128)S(1)}, u32[]{:S(2)}, u32[]{:S(2)}) %collective-permute-start.4) | collective-permute-done | bytes 524320 | tf_op jit(solution)/shard_map/ppermute | solution.py:17
  191.7 3.6 %convolution_multiply_fusion.1 = f32[128,2,512]{2,0,1:T(8,128)S(1)} fusion(f32[2,512,1536]{1,2,0:T(8,128)S(1)} %fusion.3, f32[1536,256]{1,0:T(8,128)S(1)} %constant_dynamic-update-slice_fusion), kind=kOutput, calls=%fused_computation.44 | convolution fusion | flops 2416050176 | bytes 7602176 | tf_op jit(solution)/shard_map/kgqp,pkd->qkgd/dot_general | solution.py:48
  195.4 5.5 %collective-permute-done.7 = f32[512,256]{0,1:T(8,128)S(1)} collective-permute-done((f32[512,256]{0,1:T(8,128)S(1)}, f32[512,256]{0,1:T(8,128)S(1)}, u32[]{:S(2)}, u32[]{:S(2)}) %collective-permute-start.7) | collective-permute-done | bytes 524320 | tf_op jit(solution)/shard_map/ppermute | solution.py:17
  201.0 11.1 %collective-permute-done.5 = f32[512,256]{0,1:T(8,128)S(1)} collective-permute-done((f32[512,256]{0,1:T(8,128)S(1)}, f32[512,256]{0,1:T(8,128)S(1)}, u32[]{:S(2)}, u32[]{:S(2)}) %collective-permute-start.5) | collective-permute-done | bytes 524320 | tf_op jit(solution)/shard_map/ppermute | solution.py:17
  214.7 32.6 %all_to_all.36 = f32[512,1,2,512]{3,2,1,0:T(2,128)S(1)} all-to-all(f32[512,1,2,512]{3,2,1,0:T(2,128)} %copy.120), channel_id=1, replica_groups=mesh['head'=4,'seq'=64] {'head'}, dimensions={0} | all-to-all | bytes 4194304 | tf_op jit(solution)/shard_map/all_to_all | solution.py:23
  (58 shorter events, 46.1 us)
Async XLA Ops:
  15.4 39.8 %all-to-all-start = ((f32[128,4,2,768]{3,2,0,1:T(2,128)}), f32[128,4,2,768]{3,2,0,1:T(2,128)S(1)}, u32[]{:S(2)}, u32[]{:S(2)}) async-start(f32[128,4,2,768]{3,2,0,1:T(2,128)} %copy.101), calls=%async_computation | async-start | bytes 6291456 | tf_op jit(solution)/shard_map/all_to_all | solution.py:23
  56.4 0.8 copy-start.2
  58.0 17.1 %collective-permute-start = (f32[512,256]{1,0:T(8,128)}, f32[512,256]{1,0:T(8,128)}, u32[]{:S(2)}, u32[]{:S(2)}) collective-permute-start(f32[512,256]{1,0:T(8,128)} %bitcast.247), channel_id=1, source_target_pairs={{0,1},{1,2},{2,3},{3,4},{4,5},{5,6},{6,7},{7,8},{8,9},{9,10},{10,1... | collective-permute-start | bytes 1572872 | tf_op jit(solution)/shard_map/ppermute | solution.py:17
  66.9 32.5 %copy-start.3 = (f32[512,1,2,128]{3,2,0,1:T(2,128)S(1)}, f32[512,1,2,128]{3,2,0,1:T(2,128)}, u32[]{:S(2)}) copy-start(f32[512,1,2,128]{3,2,0,1:T(2,128)} %copy-done.2) | copy-start | bytes 1572868
  66.9 32.5 %copy-start = (pred[512,1536]{0,1:T(8,128)(4,1)S(1)}, pred[512,1536]{0,1:T(8,128)(4,1)}, u32[]{:S(2)}) copy-start(pred[512,1536]{0,1:T(8,128)(4,1)} %and_and_fusion) | copy-start | bytes 2359300
  71.0 16.0 %collective-permute-start.2 = (f32[512,256]{1,0:T(8,128)S(1)}, f32[512,256]{1,0:T(8,128)S(1)}, u32[]{:S(2)}, u32[]{:S(2)}) collective-permute-start(f32[512,256]{1,0:T(8,128)S(1)} %bitcast.274), channel_id=1, source_target_pairs={{0,1},{1,2},{2,3},{3,4},{4,5},{5,6},{6,7},{7,8},{8,9},{9,10},{10,1... | collective-permute-start | bytes 1572872 | tf_op jit(solution)/shard_map/ppermute | solution.py:17
  75.1 23.1 %collective-permute-start.1 = (f32[512,256]{1,0:T(8,128)}, f32[512,256]{1,0:T(8,128)S(1)}, u32[]{:S(2)}, u32[]{:S(2)}) collective-permute-start(f32[512,256]{1,0:T(8,128)} %collective-permute-done), channel_id=1, source_target_pairs={{0,1},{1,2},{2,3},{3,4},{4,5},{5,6},{6,7},{7,8},{8,9},{9,10},{10,1... | collective-permute-start | bytes 1572872 | tf_op jit(solution)/shard_map/ppermute | solution.py:17
  87.0 46.1 %collective-permute-start.3 = (f32[512,256]{1,0:T(8,128)S(1)}, f32[512,256]{1,0:T(8,128)S(1)}, u32[]{:S(2)}, u32[]{:S(2)}) collective-permute-start(f32[512,256]{1,0:T(8,128)S(1)} %collective-permute-done.2), channel_id=1, source_target_pairs={{0,1},{1,2},{2,3},{3,4},{4,5},{5,6},{6,7},{7,8},{8,9},{9,10},{10,1... | collective-permute-start | bytes 1572872 | tf_op jit(solution)/shard_map/ppermute | solution.py:17
  122.4 10.7 %copy-start.1 = (f32[512,1,2,128]{3,2,0,1:T(2,128)S(1)}, f32[512,1,2,128]{3,2,0,1:T(2,128)}, u32[]{:S(2)}) copy-start(f32[512,1,2,128]{3,2,0,1:T(2,128)} %get-tuple-element.14) | copy-start | bytes 1572868
  130.3 48.3 %collective-permute-start.6 = (f32[512,256]{0,1:T(8,128)S(1)}, f32[512,256]{0,1:T(8,128)S(1)}, u32[]{:S(2)}, u32[]{:S(2)}) collective-permute-start(f32[512,256]{0,1:T(8,128)S(1)} %pad_maximum_fusion.3), channel_id=1, source_target_pairs={{1,0},{2,1},{3,2},{4,3},{5,4},{6,5},{7,6},{8,7},{9,8},{10,9},{11,1... | collective-permute-start | bytes 1572872 | tf_op jit(solution)/shard_map/ppermute | solution.py:17
  172.1 17.6 %collective-permute-start.4 = (f32[512,256]{0,1:T(8,128)S(1)}, f32[512,256]{0,1:T(8,128)S(1)}, u32[]{:S(2)}, u32[]{:S(2)}) collective-permute-start(f32[512,256]{0,1:T(8,128)S(1)} %pad_maximum_fusion.4), channel_id=1, source_target_pairs={{1,0},{2,1},{3,2},{4,3},{5,4},{6,5},{7,6},{8,7},{9,8},{10,9},{11,1... | collective-permute-start | bytes 1572872 | tf_op jit(solution)/shard_map/ppermute | solution.py:17
  178.8 22.1 %collective-permute-start.7 = (f32[512,256]{0,1:T(8,128)S(1)}, f32[512,256]{0,1:T(8,128)S(1)}, u32[]{:S(2)}, u32[]{:S(2)}) collective-permute-start(f32[512,256]{0,1:T(8,128)S(1)} %fusion.53), channel_id=1, source_target_pairs={{1,0},{2,1},{3,2},{4,3},{5,4},{6,5},{7,6},{8,7},{9,8},{10,9},{11,1... | collective-permute-start | bytes 1572872 | tf_op jit(solution)/shard_map/ppermute | solution.py:17
  189.7 22.3 %collective-permute-start.5 = (f32[512,256]{0,1:T(8,128)S(1)}, f32[512,256]{0,1:T(8,128)S(1)}, u32[]{:S(2)}, u32[]{:S(2)}) collective-permute-start(f32[512,256]{0,1:T(8,128)S(1)} %fusion.57), channel_id=1, source_target_pairs={{1,0},{2,1},{3,2},{4,3},{5,4},{6,5},{7,6},{8,7},{9,8},{10,9},{11,1... | collective-permute-start | bytes 1572872 | tf_op jit(solution)/shard_map/ppermute | solution.py:17
where the time goes:
time: 257 us; the launch traced here: 252 us
  matrix products  75.4 us (29%)
  waiting for transfers between devices  64.1 us (25%)
  starting transfers between devices  42.7 us (17%)
  blocking collectives  32.6 us (13%)
  local copies, waits for them, and re-layouts  30.1 us (12%)
  other arithmetic  6.11 us (2%)
    ppermute x8, starting transfers between devices, shifted(): return lax.ppermute(value, axis, pairs)  37.9 us
    all_to_all x1, waiting for transfers between devices, side_by_side(): lax.all_to_all(both, axis, split_axis=split_dim, concat_axis=concat_dim,...  35 us
    all_to_all x1, blocking collectives, side_by_side(): lax.all_to_all(both, axis, split_axis=split_dim, concat_axis=concat_dim,...  32.6 us
    ppermute x8, waiting for transfers between devices, shifted(): return lax.ppermute(value, axis, pairs)  29.1 us
    unnamed x21, local copies, waits for them, and re-layouts  16.4 us
    dot_general x2, matrix products, band_grads(): jnp.einsum('kgqp,qkgd->pkd', weights, grad_heads, precision=highest)  15.5 us
    dot_general x2, matrix products, band_grads(): jnp.einsum('qkgd,pkd->kgqp', grad_heads, value_heads, precision=highest)  14.9 us
    dot_general x2, matrix products, band_grads(): jnp.einsum('qkgd,pkd->kgqp', query_heads, key_heads, precision=highest)  13.9 us
  transfers between devices with their start and end apart: 9, of which 6 were waited for; matrix products, arithmetic and copies ran while one was open for 34% of the time, Pallas kernels for 0%

commit v1 on v0

v1 whole, which is shorter than its diff:
```python
import math

import jax
import jax.numpy as jnp
from jax import lax
from jax.experimental import pallas as pl
from jax.experimental.pallas import tpu as pltpu
from jax.sharding import PartitionSpec as P

HD = 128
TOK = 128
RING = 8
TILE = 256
TILES = 4
SPAN = TILES + 1
CHUNK = 64
LOG2E = math.log2(math.e)
LN2 = math.log(2.0)
score_scale = 168.0 ** (-0.5)
MESH = pl.DeviceIdType.MESH
f32 = jnp.float32
bf16 = jnp.bfloat16


def halves(value):
    high = value.astype(bf16)
    low = (value - high.astype(f32)).astype(bf16)
    return high, low


def dot_nt(a, b):
    return lax.dot_general(a, b, (((1,), (1,)), ((), ())), preferred_element_type=f32)


def dot_nn(a, b):
    return lax.dot_general(a, b, (((1,), (0,)), ((), ())), preferred_element_type=f32)


def kernel(
    rows,
    q_in, k_in, v_in, g_in,
    dq_out, dk_out, dv_out,
    kst, vst, qst, gst,
    k4, v4, kt, q4, q2, g4, g2,
    sbuf, pbuf, wcat, scat, scol,
    dkacc, dvacc, dqst, hk, hv, dkf, dvf,
    k_send, k_recv, v_send, v_recv, q_send, q_recv, g_send, g_recv,
    pk_send, pk_recv, pv_send, pv_recv,
    hk_send, hk_recv, hv_send, hv_recv,
    dq_send, dq_recv, dk_send, dk_recv, dv_send, dv_recv,
):
    seq = lax.axis_index("seq")
    head = lax.axis_index("head")
    row = seq // 2
    me = lax.rem(seq, 2) * 4 + head
    chip = me // 2
    core = lax.rem(me, 2)
    has_prev = row > 0
    has_next = row < rows - 1

    def device(r, p):
        return {"seq": 2 * r + p // 4, "head": lax.rem(p, 4)}

    def peer(i, sign):
        j = i // 2
        step = 3 if j == 2 else 2 if j == 3 else j
        return lax.rem(chip + 4 + sign * step, 4) * 2 + lax.rem(core + i % 2, 2)

    def source(i):
        j = i // 2
        step = jnp.where(j == 2, 3, jnp.where(j == 3, 2, j))
        return lax.rem(chip + 4 - step, 4) * 2 + lax.rem(core + lax.rem(i, 2), 2)

    def remote(src, dst, send, recv, r, p):
        return pltpu.make_async_remote_copy(
            src_ref=src, dst_ref=dst, send_sem=send, recv_sem=recv,
            device_id=device(r, p), device_id_type=MESH,
        )

    barrier = pltpu.get_barrier_semaphore()
    for i in range(1, RING):
        pl.semaphore_signal(barrier, inc=1, device_id=device(row, peer(i, 1)), device_id_type=MESH)

    @pl.when(has_prev)
    def _():
        pl.semaphore_signal(barrier, inc=1, device_id=device(row - 1, me), device_id_type=MESH)

    @pl.when(has_next)
    def _():
        pl.semaphore_signal(barrier, inc=1, device_id=device(row + 1, me), device_id_type=MESH)

    pl.semaphore_wait(barrier, RING - 1 + has_prev.astype(jnp.int32) + has_next.astype(jnp.int32))

    def columns(p, width):
        return pl.ds(pl.multiple_of(p * width, width), width)

    for src, width, stage, send, recv, first in (
        (k_in, HD, kst, k_send, k_recv, RING),
        (v_in, HD, vst, v_send, v_recv, RING),
        (q_in, 2 * HD, qst, q_send, q_recv, 0),
        (g_in, 2 * HD, gst, g_send, g_recv, 0),
    ):
        pltpu.make_async_copy(
            src.at[:, columns(me, width)], stage.at[first + me], recv.at[me]
        ).start()
    for pair in (
        ((k_in, HD, kst, k_send, k_recv, RING), (v_in, HD, vst, v_send, v_recv, RING)),
        ((q_in, 2 * HD, qst, q_send, q_recv, 0), (g_in, 2 * HD, gst, g_send, g_recv, 0)),
    ):
        for i in range(1, RING):
            for src, width, stage, send, recv, first in pair:
                to = peer(i, 1)
                remote(
                    src.at[:, columns(to, width)], stage.at[first + me],
                    send.at[to], recv.at[me], row, to,
                ).start()

    dkacc[...] = jnp.zeros_like(dkacc)
    dvacc[...] = jnp.zeros_like(dvacc)

    def landed(ref, sem):
        pltpu.make_async_copy(ref, ref, sem).wait()

    def prepare(block):
        at = pl.ds(pl.multiple_of(block * TOK, TOK), TOK)
        key = kst[block]
        high, low = halves(key)
        k4[at, :] = jnp.concatenate([high, low, high, low], axis=1)
        high, low = halves(key.T)
        kt[:, at] = jnp.concatenate([high, low], axis=0)
        high, low = halves(vst[block])
        v4[at, :] = jnp.concatenate([high, low, high, low], axis=1)

    def own_block(i, carry):
        p = source(i)
        landed(kst.at[RING + p], k_recv.at[p])
        landed(vst.at[RING + p], v_recv.at[p])

        @pl.when(has_next)
        def _():
            remote(kst.at[RING + p], kst.at[p], pk_send.at[p], pk_recv.at[p], row + 1, me).start()
            remote(vst.at[RING + p], vst.at[p], pv_send.at[p], pv_recv.at[p], row + 1, me).start()

        prepare(RING + p)
        return carry

    lax.fori_loop(0, RING, own_block, 0)

    @pl.when(has_prev)
    def _():
        def prev_block(i, carry):
            p = source(i)
            landed(kst.at[p], pk_recv.at[p])
            landed(vst.at[p], pv_recv.at[p])
            prepare(p)
            return carry

        lax.fori_loop(0, RING, prev_block, 0)

    @pl.when(jnp.logical_not(has_prev))
    def _():
        k4[: RING * TOK, :] = jnp.zeros((RING * TOK, 4 * HD), bf16)
        v4[: RING * TOK, :] = jnp.zeros((RING * TOK, 4 * HD), bf16)
        kt[:, : RING * TOK] = jnp.zeros((2 * HD, RING * TOK), bf16)

    lanes = 2 * TILE

    def query_tile(b):
        for e in range(2):
            landed(qst.at[2 * b + e], q_recv.at[2 * b + e])
            landed(gst.at[2 * b + e], g_recv.at[2 * b + e])
        for e in range(2):
            for h in range(2):
                at = slice(h * TILE + e * TOK, h * TILE + (e + 1) * TOK)
                at2 = slice(lanes + h * TILE + e * TOK, lanes + h * TILE + (e + 1) * TOK)
                cols = slice(h * HD, (h + 1) * HD)
                high, low = halves(qst[2 * b + e, :, cols] * (score_scale * LOG2E))
                q4[at, :] = jnp.concatenate([high, high, low, low], axis=1)
                both = jnp.concatenate([high, low], axis=1)
                q2[at, :] = both
                q2[at2, :] = both
                high, low = halves(gst[2 * b + e, :, cols])
                g4[at, :] = jnp.concatenate([high, high, low, low], axis=1)
                both = jnp.concatenate([high, low], axis=1)
                g2[at, :] = both
                g2[at2, :] = both

        def keys(j):
            return pl.ds(pl.multiple_of((b + j) * TILE, TILE), TILE)

        top = jnp.full((8, lanes), -1e30, f32)
        for j in range(SPAN):
            score = dot_nt(k4[keys(j), :], q4[...])
            if j in (0, SPAN - 1):
                key = lax.broadcasted_iota(jnp.int32, (TILE, lanes), 0)
                query = lax.broadcasted_iota(jnp.int32, (TILE, lanes), 1) & (TILE - 1)
                score = jnp.where(key > query if j == 0 else key <= query, score, -1e30)
            if j < SPAN - 1:
                absent = jnp.logical_and(jnp.logical_not(has_prev), b + j < TILES)
                score = score + jnp.where(absent, -1e30, 0.0)
            sbuf[j * TILE : (j + 1) * TILE, :] = score
            top = jnp.maximum(top, jnp.max(score.reshape(TILE // 8, 8, lanes), axis=0))
            pbuf[j * TILE : (j + 1) * TILE, :] = dot_nt(v4[keys(j), :], g4[...])
        top = jnp.max(top, axis=0, keepdims=True)
        total = jnp.zeros((8, lanes), f32)
        inner = jnp.zeros((8, lanes), f32)
        for n in range(SPAN * TILE // CHUNK):
            at = slice(n * CHUNK, (n + 1) * CHUNK)
            raised = jnp.exp2(sbuf[at, :] - top)
            sbuf[at, :] = raised
            total = total + jnp.sum(raised.reshape(CHUNK // 8, 8, lanes), axis=0)
            inner = inner + jnp.sum((raised * pbuf[at, :]).reshape(CHUNK // 8, 8, lanes), axis=0)
        inverse = 1.0 / jnp.sum(total, axis=0, keepdims=True)
        inner = jnp.sum(inner, axis=0, keepdims=True) * inverse
        turned = jnp.zeros((2 * HD, lanes), f32)
        for j in range(SPAN):
            for n in range(TILE // CHUNK):
                at = slice(j * TILE + n * CHUNK, j * TILE + (n + 1) * CHUNK)
                to = slice(n * CHUNK, (n + 1) * CHUNK)
                weight = sbuf[at, :] * inverse
                slope = weight * (pbuf[at, :] - inner)
                high, low = halves(weight)
                wcat[j % 2, to, :lanes] = high
                wcat[j % 2, to, lanes:] = low
                high, low = halves(slope)
                scat[j % 2, to, :lanes] = high
                scat[j % 2, to, lanes:] = low
            part = dot_nn(wcat[j % 2], g2[...])
            dvacc[keys(j), :] += part[:, :HD] + part[:, HD:]
            part = dot_nn(scat[j % 2], q2[...])
            dkacc[keys(j), :] += part[:, :HD] + part[:, HD:]
            turned = turned + dot_nn(kt[:, keys(j)], scat[j % 2, :, :lanes])
            turned = turned + dot_nn(kt[:, keys(j)], scat[j % 2, :, lanes:])
        grad = (turned[:HD] + turned[HD:]) * score_scale
        for e in range(2):
            to = 2 * b + e
            for h in range(2):
                part = grad[:, h * TILE + e * TOK : h * TILE + (e + 1) * TOK]
                dqst[to, :, h * HD : (h + 1) * HD] = part.T

            @pl.when(to == me)
            def _():
                pltpu.make_async_copy(dqst.at[to], dq_out.at[:, columns(me, 2 * HD)], dq_recv.at[me]).start()

            @pl.when(to != me)
            def _():
                remote(
                    dqst.at[to], dq_out.at[:, columns(me, 2 * HD)],
                    dq_send.at[to], dq_recv.at[me], row, to,
                ).start()

    def tile_rows(t):
        return pl.ds(pl.multiple_of(t * TILE, TILE), TILE)

    def send_back(t):
        @pl.when(has_prev)
        def _():
            remote(dkacc.at[tile_rows(t)], hk.at[t], hk_send.at[t], hk_recv.at[t], row - 1, me).start()
            remote(dvacc.at[tile_rows(t)], hv.at[t], hv_send.at[t], hv_recv.at[t], row - 1, me).start()

    def step(i, carry):
        b = jnp.where(i == 0, chip, jnp.where(i <= chip, i - 1, i))
        query_tile(b)
        for t in range(TILES):
            ready = jnp.where(t < chip, t + 1, t)

            @pl.when(i == ready)
            def _():
                send_back(t)
        return carry

    lax.fori_loop(0, TILES, step, 0)

    def finish(t, carry):
        @pl.when(has_next)
        def _():
            landed(hk.at[t], hk_recv.at[t])
            landed(hv.at[t], hv_recv.at[t])

        @pl.when(jnp.logical_not(has_next))
        def _():
            hk[t] = jnp.zeros((TILE, HD), f32)
            hv[t] = jnp.zeros((TILE, HD), f32)

        own = pl.ds(pl.multiple_of(RING * TOK + t * TILE, TILE), TILE)
        dkf[t] = (dkacc[own, :] + hk[t]) * LN2
        dvf[t] = dvacc[own, :] + hv[t]
        for e in range(2):
            to = 2 * t + e
            part = slice(e * TOK, (e + 1) * TOK)

            @pl.when(to == me)
            def _():
                pltpu.make_async_copy(dkf.at[t, part], dk_out.at[:, columns(me, HD)], dk_recv.at[me]).start()
                pltpu.make_async_copy(dvf.at[t, part], dv_out.at[:, columns(me, HD)], dv_recv.at[me]).start()

            @pl.when(to != me)
            def _():
                remote(dkf.at[t, part], dk_out.at[:, columns(me, HD)], dk_send.at[to], dk_recv.at[me], row, to).start()
                remote(dvf.at[t, part], dv_out.at[:, columns(me, HD)], dv_send.at[to], dv_recv.at[me], row, to).start()
        return carry

    lax.fori_loop(0, TILES, finish, 0)

    def sent(p, carry):
        @pl.when(p != me)
        def _():
            landed(kst.at[RING + me], k_send.at[p])
            landed(vst.at[RING + me], v_send.at[p])
            landed(qst.at[me], q_send.at[p])
            landed(gst.at[me], g_send.at[p])
            landed(dqst.at[p], dq_send.at[p])
            landed(dkf.at[0, :TOK], dk_send.at[p])
            landed(dvf.at[0, :TOK], dv_send.at[p])

        @pl.when(has_next)
        def _():
            landed(kst.at[RING + p], pk_send.at[p])
            landed(vst.at[RING + p], pv_send.at[p])

        return carry

    lax.fori_loop(0, RING, sent, 0)

    @pl.when(has_prev)
    def _():
        def halo_sent(t, carry):
            landed(dkacc.at[tile_rows(t)], hk_send.at[t])
            landed(dvacc.at[tile_rows(t)], hv_send.at[t])
            return carry

        lax.fori_loop(0, TILES, halo_sent, 0)

    def got(p, carry):
        landed(dq_out.at[:, columns(p, 2 * HD)], dq_recv.at[p])
        landed(dk_out.at[:, columns(p, HD)], dk_recv.at[p])
        landed(dv_out.at[:, columns(p, HD)], dv_recv.at[p])
        return carry

    lax.fori_loop(0, RING, got, 0)


def solution(mesh):
    rows = mesh.shape["seq"] // 2

    def per_device(query, key_in, value_in, d_out):
        lanes = 2 * TILE
        all_keys = 2 * RING * TOK
        dma = pltpu.SemaphoreType.DMA
        return pl.pallas_call(
            lambda *refs: kernel(rows, *refs),
            out_shape=(
                jax.ShapeDtypeStruct(query.shape, f32),
                jax.ShapeDtypeStruct(key_in.shape, f32),
                jax.ShapeDtypeStruct(value_in.shape, f32),
            ),
            in_specs=[pl.BlockSpec(memory_space=pl.ANY)] * 4,
            out_specs=[pl.BlockSpec(memory_space=pl.ANY)] * 3,
            scratch_shapes=[
                pltpu.VMEM((2 * RING, TOK, HD), f32),
                pltpu.VMEM((2 * RING, TOK, HD), f32),
                pltpu.VMEM((RING, TOK, 2 * HD), f32),
                pltpu.VMEM((RING, TOK, 2 * HD), f32),
                pltpu.VMEM((all_keys, 4 * HD), bf16),
                pltpu.VMEM((all_keys, 4 * HD), bf16),
                pltpu.VMEM((2 * HD, all_keys), bf16),
                pltpu.VMEM((lanes, 4 * HD), bf16),
                pltpu.VMEM((2 * lanes, 2 * HD), bf16),
                pltpu.VMEM((lanes, 4 * HD), bf16),
                pltpu.VMEM((2 * lanes, 2 * HD), bf16),
                pltpu.VMEM((SPAN * TILE, lanes), f32),
                pltpu.VMEM((SPAN * TILE, lanes), f32),
                pltpu.VMEM((2, TILE, 2 * lanes), bf16),
                pltpu.VMEM((2, TILE, 2 * lanes), bf16),
                pltpu.VMEM((8, 128), f32),
                pltpu.VMEM((all_keys, HD), f32),
                pltpu.VMEM((all_keys, HD), f32),
                pltpu.VMEM((RING, TOK, 2 * HD), f32),
                pltpu.VMEM((TILES, TILE, HD), f32),
                pltpu.VMEM((TILES, TILE, HD), f32),
                pltpu.VMEM((TILES, TILE, HD), f32),
                pltpu.VMEM((TILES, TILE, HD), f32),
            ]
            + [dma((RING,))] * 12
            + [dma((TILES,))] * 4
            + [dma((RING,))] * 6,
            compiler_params=pltpu.CompilerParams(
                collective_id=0, has_side_effects=True, vmem_limit_bytes=48 * 2**20
            ),
            cost_estimate=pl.CostEstimate(
                flops=5 * 2 * 2 * 1024 * 1280 * HD, bytes_accessed=6 * 2**20, transcendentals=2 * 1024 * 1280
            ),
        )(query, key_in, value_in, d_out)

    spec = P(("seq", "head"), None)
    return jax.shard_map(
        per_device, mesh=mesh, in_specs=(spec,) * 4, out_specs=(spec,) * 3, check_vma=False
    )
```

time: 257 us -> 85.5 us (0.33); the launches traced: 252 us -> 85.2 us
  Pallas kernels: 0 us -> 77.5 us
  matrix products: 75.4 us -> 0 us
  waiting for transfers between devices: 64.1 us -> 0 us
  starting transfers between devices: 42.7 us -> 0 us
  blocking collectives: 32.6 us -> 0 us
  local copies, waits for them, and re-layouts: 30.1 us -> 7.08 us
  other arithmetic: 6.11 us -> 0 us
    pallas_call x0 -> x1, Pallas kernels: none -> 77.5 us  [per_device(): pl.pallas_call(lambda *refs: kernel(rows, *refs), out_shape=(jax.ShapeDty...]
    dot_general x12 -> x0, matrix products: 75.4 us -> none  [the longest x2 15.5 us: band_grads(): jnp.einsum('kgqp,qkgd->pkd', weights, grad_heads, precision=highest)]
    ppermute x8 -> x0, starting transfers between devices: 37.9 us -> none  [shifted(): return lax.ppermute(value, axis, pairs)]
    all_to_all x1 -> x0, waiting for transfers between devices: 35 us -> none  [side_by_side(): lax.all_to_all(both, axis, split_axis=split_dim, concat_axis=concat_dim,...]
    all_to_all x1 -> x0, blocking collectives: 32.6 us -> none  [side_by_side(): lax.all_to_all(both, axis, split_axis=split_dim, concat_axis=concat_dim,...]
    ppermute x8 -> x0, waiting for transfers between devices: 29.1 us -> none  [shifted(): return lax.ppermute(value, axis, pairs)]
    unnamed x21 -> x11, local copies, waits for them, and re-layouts: 16.4 us -> 7.08 us
    split x9 -> x0, local copies, waits for them, and re-layouts: 7.15 us -> none  [side_by_side(): jnp.split(whole, [sum(widths[:k]) for k in range(1, len(widths))], axis=a...]
  transfers between devices with their start and end apart: 9 -> 0, of which waited for: 6 -> 0; matrix products, arithmetic and copies ran while one was open for 34% -> 0% of each run, Pallas kernels for 0% -> 0%
where the time goes in v1:
time: 85.5 us; the launch traced here: 85.2 us
  Pallas kernels  77.5 us (91%)
  local copies, waits for them, and re-layouts  7.08 us (8%)
    pallas_call x1, Pallas kernels, per_device(): pl.pallas_call(lambda *refs: kernel(rows, *refs), out_shape=(jax.ShapeDty...  77.5 us
    unnamed x11, local copies, waits for them, and re-layouts  7.08 us

profile of v1, /device:TPU:127, one launch (start us, length us, event | category | flops | bytes accessed | tf_op | source)
XLA Modules:
  0.0 85.2 jit_solution(1399811259380174634)
XLA Ops:
  0.6 0.0 copy-start
  0.6 1.2 %copy-done = f32[128,2048]{1,0:T(8,128)S(1)} copy-done((f32[128,2048]{1,0:T(8,128)S(1)}, f32[128,2048]{1,0:T(8,128)}, u32[]{:S(2)}) %copy-start) | copy-done | bytes 1048600
  1.9 0.0 copy-start.1
  1.9 1.2 %copy-done.1 = f32[128,2048]{1,0:T(8,128)S(1)} copy-done((f32[128,2048]{1,0:T(8,128)S(1)}, f32[128,2048]{1,0:T(8,128)}, u32[]{:S(2)}) %copy-start.1) | copy-done | bytes 1048600
  3.1 0.0 copy-start.2
  3.1 1.0 %copy-done.2 = f32[128,1024]{1,0:T(8,128)S(1)} copy-done((f32[128,1024]{1,0:T(8,128)S(1)}, f32[128,1024]{1,0:T(8,128)}, u32[]{:S(2)}) %copy-start.2) | copy-done | bytes 524312
  4.1 0.0 copy-start.3
  4.1 1.0 %copy-done.3 = f32[128,1024]{1,0:T(8,128)S(1)} copy-done((f32[128,1024]{1,0:T(8,128)S(1)}, f32[128,1024]{1,0:T(8,128)}, u32[]{:S(2)}) %copy-start.3) | copy-done | bytes 524312
  5.2 77.5 %shard_map.67 = (f32[128,2048]{1,0:T(8,128)S(1)}, f32[128,1024]{1,0:T(8,128)S(1)}, f32[128,1024]{1,0:T(8,128)S(1)}) custom-call(f32[128,2048]{1,0:T(8,128)S(1)} %copy-done, f32[128,1024]{1,0:T(8,128)S(1)} %copy-done.2, f32[128,1024]{1,0:T(8,128)S(1)} %copy-done.3, f32[128,2048]{1,0:T(8,128)S(1)} %copy-done.1), custom_call_target="tpu_custom_call" | custom-call | flops 3355443200 | bytes 6291456 | tf_op jit(solution)/shard_map/pallas_call | solution.py:350
  82.7 1.0 %copy.10 = f32[128,2048]{1,0:T(8,128)} copy(f32[128,2048]{1,0:T(8,128)S(1)} %get-tuple-element.6) | data formatting | bytes 2097152
  83.6 0.8 copy.11
  84.4 0.8 copy.12
Async XLA Ops:
  0.6 1.2 %copy-start = (f32[128,2048]{1,0:T(8,128)S(1)}, f32[128,2048]{1,0:T(8,128)}, u32[]{:S(2)}) copy-start(f32[128,2048]{1,0:T(8,128)} %refs_0_.1) | copy-start | bytes 3145732
  1.9 1.2 %copy-start.1 = (f32[128,2048]{1,0:T(8,128)S(1)}, f32[128,2048]{1,0:T(8,128)}, u32[]{:S(2)}) copy-start(f32[128,2048]{1,0:T(8,128)} %refs_3_.1) | copy-start | bytes 3145732
  3.1 1.0 %copy-start.2 = (f32[128,1024]{1,0:T(8,128)S(1)}, f32[128,1024]{1,0:T(8,128)}, u32[]{:S(2)}) copy-start(f32[128,1024]{1,0:T(8,128)} %refs_1_.1) | copy-start | bytes 1572868
  4.1 1.0 %copy-start.3 = (f32[128,1024]{1,0:T(8,128)S(1)}, f32[128,1024]{1,0:T(8,128)}, u32[]{:S(2)}) copy-start(f32[128,1024]{1,0:T(8,128)} %refs_2_.1) | copy-start | bytes 1572868

commit v2 on v1

--- a/solution.py
+++ b/solution.py
@@ -16,6 +16,7 @@
 CHUNK = 64
 LOG2E = math.log2(math.e)
 LN2 = math.log(2.0)
+ORDER = ((0, 1, 3, 2), (1, 0, 2, 3), (2, 0, 1, 3), (3, 0, 2, 1))
 score_scale = 168.0 ** (-0.5)
 MESH = pl.DeviceIdType.MESH
 f32 = jnp.float32
@@ -42,7 +43,7 @@
     dq_out, dk_out, dv_out,
     kst, vst, qst, gst,
     k4, v4, kt, q4, q2, g4, g2,
-    sbuf, pbuf, wcat, scat, scol,
+    sbuf, pbuf, wcat, scat,
     dkacc, dvacc, dqst, hk, hv, dkf, dvf,
     k_send, k_recv, v_send, v_recv, q_send, q_recv, g_send, g_recv,
     pk_send, pk_recv, pv_send, pv_recv,
@@ -58,6 +59,16 @@
     has_prev = row > 0
     has_next = row < rows - 1
 
+    def by_chip(table):
+        lines = [sum(n << (2 * k) for k, n in enumerate(line)) for line in table]
+        code = lines[TILES - 1]
+        for c in range(TILES - 2, -1, -1):
+            code = jnp.where(chip == c, lines[c], code)
+        return code
+
+    order = by_chip(ORDER)
+    ready = by_chip([[max(line.index(n) for n in range(t + 1)) for t in range(TILES)] for line in ORDER])
+
     def device(r, p):
         return {"seq": 2 * r + p // 4, "head": lax.rem(p, 4)}
 
@@ -67,9 +78,7 @@
         return lax.rem(chip + 4 + sign * step, 4) * 2 + lax.rem(core + i % 2, 2)
 
     def source(i):
-        j = i // 2
-        step = jnp.where(j == 2, 3, jnp.where(j == 3, 2, j))
-        return lax.rem(chip + 4 - step, 4) * 2 + lax.rem(core + lax.rem(i, 2), 2)
+        return lax.rem(chip + i // 2, 4) * 2 + lax.rem(core + lax.rem(i, 2), 2)
 
     def remote(src, dst, send, recv, r, p):
         return pltpu.make_async_remote_copy(
@@ -103,17 +112,18 @@
         pltpu.make_async_copy(
             src.at[:, columns(me, width)], stage.at[first + me], recv.at[me]
         ).start()
-    for pair in (
-        ((k_in, HD, kst, k_send, k_recv, RING), (v_in, HD, vst, v_send, v_recv, RING)),
-        ((q_in, 2 * HD, qst, q_send, q_recv, 0), (g_in, 2 * HD, gst, g_send, g_recv, 0)),
-    ):
-        for i in range(1, RING):
+    def spread(pair, offsets):
+        for i in offsets:
             for src, width, stage, send, recv, first in pair:
                 to = peer(i, 1)
                 remote(
                     src.at[:, columns(to, width)], stage.at[first + me],
                     send.at[to], recv.at[me], row, to,
                 ).start()
+
+    keys_values = ((k_in, HD, kst, k_send, k_recv, RING), (v_in, HD, vst, v_send, v_recv, RING))
+    queries = ((q_in, 2 * HD, qst, q_send, q_recv, 0), (g_in, 2 * HD, gst, g_send, g_recv, 0))
+    spread(keys_values, range(1, RING))
 
     dkacc[...] = jnp.zeros_like(dkacc)
     dvacc[...] = jnp.zeros_like(dvacc)
@@ -144,10 +154,16 @@
         prepare(RING + p)
         return carry
 
-    lax.fori_loop(0, RING, own_block, 0)
-
-    @pl.when(has_prev)
-    def _():
+    lax.fori_loop(0, 4, own_block, 0)
+    spread(queries, range(1, 6))
+
+    @pl.when(chip == 0)
+    def _():
+        spread(queries, range(6, RING))
+
+    lax.fori_loop(4, RING, own_block, 0)
+
+    def prev_blocks(first, last):
         def prev_block(i, carry):
             p = source(i)
             landed(kst.at[p], pk_recv.at[p])
@@ -155,7 +171,16 @@
             prepare(p)
             return carry
 
-        lax.fori_loop(0, RING, prev_block, 0)
+        @pl.when(has_prev)
+        def _():
+            lax.fori_loop(first, last, prev_block, 0)
+
+    early = RING - 2 * chip
+    prev_blocks(0, early)
+
+    @pl.when(chip != 0)
+    def _():
+        spread(queries, range(6, RING))
 
     @pl.when(jnp.logical_not(has_prev))
     def _():
@@ -249,58 +274,60 @@
                     dq_send.at[to], dq_recv.at[me], row, to,
                 ).start()
 
-    def tile_rows(t):
-        return pl.ds(pl.multiple_of(t * TILE, TILE), TILE)
+    def block_rows(p):
+        return pl.ds(pl.multiple_of(p * TOK, TOK), TOK)
 
     def send_back(t):
         @pl.when(has_prev)
         def _():
-            remote(dkacc.at[tile_rows(t)], hk.at[t], hk_send.at[t], hk_recv.at[t], row - 1, me).start()
-            remote(dvacc.at[tile_rows(t)], hv.at[t], hv_send.at[t], hv_recv.at[t], row - 1, me).start()
+            for p in (2 * t, 2 * t + 1):
+                remote(dkacc.at[block_rows(p)], hk.at[p], hk_send.at[p], hk_recv.at[p], row - 1, me).start()
+                remote(dvacc.at[block_rows(p)], hv.at[p], hv_send.at[p], hv_recv.at[p], row - 1, me).start()
 
     def step(i, carry):
-        b = jnp.where(i == 0, chip, jnp.where(i <= chip, i - 1, i))
+        b = (order >> (2 * i)) & 3
+
+        @pl.when(i == 1)
+        def _():
+            prev_blocks(early, RING)
+
         query_tile(b)
         for t in range(TILES):
-            ready = jnp.where(t < chip, t + 1, t)
-
-            @pl.when(i == ready)
+            @pl.when(i == (ready >> (2 * t)) & 3)
             def _():
                 send_back(t)
         return carry
 
     lax.fori_loop(0, TILES, step, 0)
 
-    def finish(t, carry):
+    def finish(to, carry):
         @pl.when(has_next)
         def _():
-            landed(hk.at[t], hk_recv.at[t])
-            landed(hv.at[t], hv_recv.at[t])
+            landed(hk.at[to], hk_recv.at[to])
+            landed(hv.at[to], hv_recv.at[to])
 
         @pl.when(jnp.logical_not(has_next))
         def _():
-            hk[t] = jnp.zeros((TILE, HD), f32)
-            hv[t] = jnp.zeros((TILE, HD), f32)
-
-        own = pl.ds(pl.multiple_of(RING * TOK + t * TILE, TILE), TILE)
-        dkf[t] = (dkacc[own, :] + hk[t]) * LN2
-        dvf[t] = dvacc[own, :] + hv[t]
-        for e in range(2):
-            to = 2 * t + e
-            part = slice(e * TOK, (e + 1) * TOK)
-
-            @pl.when(to == me)
-            def _():
-                pltpu.make_async_copy(dkf.at[t, part], dk_out.at[:, columns(me, HD)], dk_recv.at[me]).start()
-                pltpu.make_async_copy(dvf.at[t, part], dv_out.at[:, columns(me, HD)], dv_recv.at[me]).start()
-
-            @pl.when(to != me)
-            def _():
-                remote(dkf.at[t, part], dk_out.at[:, columns(me, HD)], dk_send.at[to], dk_recv.at[me], row, to).start()
-                remote(dvf.at[t, part], dv_out.at[:, columns(me, HD)], dv_send.at[to], dv_recv.at[me], row, to).start()
+            hk[to] = jnp.zeros((TOK, HD), f32)
+            hv[to] = jnp.zeros((TOK, HD), f32)
+
+        own = block_rows(RING + to)
+        dkf[to] = (dkacc[own, :] + hk[to]) * LN2
+        dvf[to] = dvacc[own, :] + hv[to]
+
+        @pl.when(to == me)
+        def _():
+            pltpu.make_async_copy(dkf.at[to], dk_out.at[:, columns(me, HD)], dk_recv.at[me]).start()
+            pltpu.make_async_copy(dvf.at[to], dv_out.at[:, columns(me, HD)], dv_recv.at[me]).start()
+
+        @pl.when(to != me)
+        def _():
+            remote(dkf.at[to], dk_out.at[:, columns(me, HD)], dk_send.at[to], dk_recv.at[me], row, to).start()
+            remote(dvf.at[to], dv_out.at[:, columns(me, HD)], dv_send.at[to], dv_recv.at[me], row, to).start()
+
         return carry
 
-    lax.fori_loop(0, TILES, finish, 0)
+    lax.fori_loop(0, RING, finish, 0)
 
     def sent(p, carry):
         @pl.when(p != me)
@@ -310,8 +337,8 @@
             landed(qst.at[me], q_send.at[p])
             landed(gst.at[me], g_send.at[p])
             landed(dqst.at[p], dq_send.at[p])
-            landed(dkf.at[0, :TOK], dk_send.at[p])
-            landed(dvf.at[0, :TOK], dv_send.at[p])
+            landed(dkf.at[p], dk_send.at[p])
+            landed(dvf.at[p], dv_send.at[p])
 
         @pl.when(has_next)
         def _():
@@ -324,12 +351,12 @@
 
     @pl.when(has_prev)
     def _():
-        def halo_sent(t, carry):
-            landed(dkacc.at[tile_rows(t)], hk_send.at[t])
-            landed(dvacc.at[tile_rows(t)], hv_send.at[t])
+        def halo_sent(p, carry):
+            landed(dkacc.at[block_rows(p)], hk_send.at[p])
+            landed(dvacc.at[block_rows(p)], hv_send.at[p])
             return carry
 
-        lax.fori_loop(0, TILES, halo_sent, 0)
+        lax.fori_loop(0, RING, halo_sent, 0)
 
     def got(p, carry):
         landed(dq_out.at[:, columns(p, 2 * HD)], dq_recv.at[p])
@@ -372,20 +399,17 @@
                 pltpu.VMEM((SPAN * TILE, lanes), f32),
                 pltpu.VMEM((2, TILE, 2 * lanes), bf16),
                 pltpu.VMEM((2, TILE, 2 * lanes), bf16),
-                pltpu.VMEM((8, 128), f32),
                 pltpu.VMEM((all_keys, HD), f32),
                 pltpu.VMEM((all_keys, HD), f32),
                 pltpu.VMEM((RING, TOK, 2 * HD), f32),
-                pltpu.VMEM((TILES, TILE, HD), f32),
-                pltpu.VMEM((TILES, TILE, HD), f32),
-                pltpu.VMEM((TILES, TILE, HD), f32),
-                pltpu.VMEM((TILES, TILE, HD), f32),
+                pltpu.VMEM((RING, TOK, HD), f32),
+                pltpu.VMEM((RING, TOK, HD), f32),
+                pltpu.VMEM((RING, TOK, HD), f32),
+                pltpu.VMEM((RING, TOK, HD), f32),
             ]
-            + [dma((RING,))] * 12
-            + [dma((TILES,))] * 4
-            + [dma((RING,))] * 6,
+            + [dma((RING,))] * 22,
             compiler_params=pltpu.CompilerParams(
-                collective_id=0, has_side_effects=True, vmem_limit_bytes=48 * 2**20
+                collective_id=0, has_side_effects=True, vmem_limit_bytes=60 * 2**20
             ),
             cost_estimate=pl.CostEstimate(
                 flops=5 * 2 * 2 * 1024 * 1280 * HD, bytes_accessed=6 * 2**20, transcendentals=2 * 1024 * 1280

time: 85.5 us -> 80.5 us (0.942)
  local copies, waits for them, and re-layouts: 7.08 us -> 4.38 us
  Pallas kernels: 77.5 us -> 75.3 us
    unnamed x11 -> x7, local copies, waits for them, and re-layouts: 7.08 us -> 4.38 us
    pallas_call x1, Pallas kernels: 77.5 us -> 75.3 us  [per_device(): pl.pallas_call(lambda *refs: kernel(rows, *refs), out_shape=(jax.ShapeDty...]
where the time goes in v2:
time: 80.5 us; the launch traced here: 80.3 us
  Pallas kernels  75.3 us (94%)
  local copies, waits for them, and re-layouts  4.38 us (5%)
    pallas_call x1, Pallas kernels, per_device(): pl.pallas_call(lambda *refs: kernel(rows, *refs), out_shape=(jax.ShapeDty...  75.3 us
    unnamed x7, local copies, waits for them, and re-layouts  4.38 us

profile of v2, /device:TPU:127, one launch (start us, length us, event | category | flops | bytes accessed | tf_op | source)
XLA Modules:
  0.0 80.3 jit_solution(8454576173620036593)
XLA Ops:
  0.6 75.3 %shard_map.67 = (f32[128,2048]{1,0:T(8,128)}, f32[128,1024]{1,0:T(8,128)}, f32[128,1024]{1,0:T(8,128)}) custom-call(f32[128,2048]{1,0:T(8,128)} %refs_0_.1, f32[128,1024]{1,0:T(8,128)} %refs_1_.1, f32[128,1024]{1,0:T(8,128)} %refs_2_.1, f32[128,2048]{1,0:T(8,128)} %refs_3_.1), custom_call_target="tpu_custom_call" | custom-call | flops 3355443200 | bytes 6291456 | tf_op jit(solution)/shard_map/pallas_call | solution.py:377
  76.0 0.0 copy-start.1
  76.0 2.4 %copy.10 = f32[128,2048]{1,0:T(8,128)} copy(f32[128,2048]{1,0:T(8,128)} %get-tuple-element.6) | data formatting | bytes 2097152
  78.3 0.0 copy-done.1
  78.3 0.0 copy-start
  78.3 0.8 copy.11
  79.1 0.4 copy-done
  79.5 0.8 copy.12
Async XLA Ops:
  76.0 2.4 %copy-start.1 = (f32[128,1024]{1,0:T(8,128)S(1)}, f32[128,1024]{1,0:T(8,128)}, u32[]{:S(2)}) copy-start(f32[128,1024]{1,0:T(8,128)} %get-tuple-element.7) | copy-start | bytes 1572868
  78.3 1.2 %copy-start = (f32[128,1024]{1,0:T(8,128)S(1)}, f32[128,1024]{1,0:T(8,128)}, u32[]{:S(2)}) copy-start(f32[128,1024]{1,0:T(8,128)} %get-tuple-element.8) | copy-start | bytes 1572868

commit v3 on v2

--- a/solution.py
+++ b/solution.py
@@ -16,7 +16,7 @@
 CHUNK = 64
 LOG2E = math.log2(math.e)
 LN2 = math.log(2.0)
-ORDER = ((0, 1, 3, 2), (1, 0, 2, 3), (2, 0, 1, 3), (3, 0, 2, 1))
+ORDER = ((0, 1, 3, 2), (1, 0, 2, 3), (2, 3, 0, 1), (3, 0, 2, 1))
 score_scale = 168.0 ** (-0.5)
 MESH = pl.DeviceIdType.MESH
 f32 = jnp.float32
@@ -125,6 +125,11 @@
     queries = ((q_in, 2 * HD, qst, q_send, q_recv, 0), (g_in, 2 * HD, gst, g_send, g_recv, 0))
     spread(keys_values, range(1, RING))
 
+    @pl.when(chip == 0)
+    def _():
+        spread(queries, range(1, RING))
+
+
     dkacc[...] = jnp.zeros_like(dkacc)
     dvacc[...] = jnp.zeros_like(dvacc)
 
@@ -155,11 +160,10 @@
         return carry
 
     lax.fori_loop(0, 4, own_block, 0)
-    spread(queries, range(1, 6))
-
-    @pl.when(chip == 0)
-    def _():
-        spread(queries, range(6, RING))
+
+    @pl.when(chip != 0)
+    def _():
+        spread(queries, range(1, 6))
 
     lax.fori_loop(4, RING, own_block, 0)
 
@@ -188,9 +192,19 @@
         v4[: RING * TOK, :] = jnp.zeros((RING * TOK, 4 * HD), bf16)
         kt[:, : RING * TOK] = jnp.zeros((2 * HD, RING * TOK), bf16)
 
+    def block_rows(p):
+        return pl.ds(pl.multiple_of(p * TOK, TOK), TOK)
+
+    def send_back(t):
+        @pl.when(has_prev)
+        def _():
+            for p in (2 * t, 2 * t + 1):
+                remote(dkacc.at[block_rows(p)], hk.at[p], hk_send.at[p], hk_recv.at[p], row - 1, me).start()
+                remote(dvacc.at[block_rows(p)], hv.at[p], hv_send.at[p], hv_recv.at[p], row - 1, me).start()
+
     lanes = 2 * TILE
 
-    def query_tile(b):
+    def query_tile(b, i):
         for e in range(2):
             landed(qst.at[2 * b + e], q_recv.at[2 * b + e])
             landed(gst.at[2 * b + e], g_recv.at[2 * b + e])
@@ -254,6 +268,11 @@
             dvacc[keys(j), :] += part[:, :HD] + part[:, HD:]
             part = dot_nn(scat[j % 2], q2[...])
             dkacc[keys(j), :] += part[:, :HD] + part[:, HD:]
+            if j == 0:
+                @pl.when(i == (ready >> (2 * b)) & 3)
+                def _():
+                    send_back(b)
+
             turned = turned + dot_nn(kt[:, keys(j)], scat[j % 2, :, :lanes])
             turned = turned + dot_nn(kt[:, keys(j)], scat[j % 2, :, lanes:])
         grad = (turned[:HD] + turned[HD:]) * score_scale
@@ -274,16 +293,6 @@
                     dq_send.at[to], dq_recv.at[me], row, to,
                 ).start()
 
-    def block_rows(p):
-        return pl.ds(pl.multiple_of(p * TOK, TOK), TOK)
-
-    def send_back(t):
-        @pl.when(has_prev)
-        def _():
-            for p in (2 * t, 2 * t + 1):
-                remote(dkacc.at[block_rows(p)], hk.at[p], hk_send.at[p], hk_recv.at[p], row - 1, me).start()
-                remote(dvacc.at[block_rows(p)], hv.at[p], hv_send.at[p], hv_recv.at[p], row - 1, me).start()
-
     def step(i, carry):
         b = (order >> (2 * i)) & 3
 
@@ -291,9 +300,9 @@
         def _():
             prev_blocks(early, RING)
 
-        query_tile(b)
+        query_tile(b, i)
         for t in range(TILES):
-            @pl.when(i == (ready >> (2 * t)) & 3)
+            @pl.when(jnp.logical_and(t != b, i == (ready >> (2 * t)) & 3))
             def _():
                 send_back(t)
         return carry

time: 80.5 us -> 79 us (0.981)
  Pallas kernels: 75.3 us -> 73.5 us
    pallas_call x1, Pallas kernels: 75.3 us -> 73.5 us  [per_device(): pl.pallas_call(lambda *refs: kernel(rows, *refs), out_shape=(jax.ShapeDty...]
where the time goes in v3:
time: 79 us; the launch traced here: 78.5 us
  Pallas kernels  73.5 us (93%)
  local copies, waits for them, and re-layouts  4.38 us (6%)
    pallas_call x1, Pallas kernels, per_device(): pl.pallas_call(lambda *refs: kernel(rows, *refs), out_shape=(jax.ShapeDty...  73.5 us
    unnamed x7, local copies, waits for them, and re-layouts  4.38 us

profile of v3, /device:TPU:127, one launch (start us, length us, event | category | flops | bytes accessed | tf_op | source)
XLA Modules:
  0.0 78.5 jit_solution(15145263888105390044)
XLA Ops:
  0.6 73.5 %shard_map.67 = (f32[128,2048]{1,0:T(8,128)}, f32[128,1024]{1,0:T(8,128)}, f32[128,1024]{1,0:T(8,128)}) custom-call(f32[128,2048]{1,0:T(8,128)} %refs_0_.1, f32[128,1024]{1,0:T(8,128)} %refs_1_.1, f32[128,1024]{1,0:T(8,128)} %refs_2_.1, f32[128,2048]{1,0:T(8,128)} %refs_3_.1), custom_call_target="tpu_custom_call" | custom-call | flops 3355443200 | bytes 6291456 | tf_op jit(solution)/shard_map/pallas_call | solution.py:386
  74.1 0.0 copy-start.1
  74.1 2.4 %copy.10 = f32[128,2048]{1,0:T(8,128)} copy(f32[128,2048]{1,0:T(8,128)} %get-tuple-element.6) | data formatting | bytes 2097152
  76.5 0.0 copy-done.1
  76.5 0.0 copy-start
  76.5 0.8 %copy.11 = f32[128,1024]{1,0:T(8,128)} copy(f32[128,1024]{1,0:T(8,128)S(1)} %copy-done.1) | data formatting | bytes 1048576
  77.3 0.4 copy-done
  77.7 0.8 %copy.12 = f32[128,1024]{1,0:T(8,128)} copy(f32[128,1024]{1,0:T(8,128)S(1)} %copy-done) | data formatting | bytes 1048576
Async XLA Ops:
  74.1 2.4 %copy-start.1 = (f32[128,1024]{1,0:T(8,128)S(1)}, f32[128,1024]{1,0:T(8,128)}, u32[]{:S(2)}) copy-start(f32[128,1024]{1,0:T(8,128)} %get-tuple-element.7) | copy-start | bytes 1572868
  76.5 1.2 %copy-start = (f32[128,1024]{1,0:T(8,128)S(1)}, f32[128,1024]{1,0:T(8,128)}, u32[]{:S(2)}) copy-start(f32[128,1024]{1,0:T(8,128)} %get-tuple-element.8) | copy-start | bytes 1572868

commit v4 on v3

--- a/solution.py
+++ b/solution.py
@@ -16,7 +16,7 @@
 CHUNK = 64
 LOG2E = math.log2(math.e)
 LN2 = math.log(2.0)
-ORDER = ((0, 1, 3, 2), (1, 0, 2, 3), (2, 3, 0, 1), (3, 0, 2, 1))
+ORDER = ((0, 1, 3, 2), (1, 0, 2, 3), (2, 3, 0, 1), (3, 2, 0, 1))
 score_scale = 168.0 ** (-0.5)
 MESH = pl.DeviceIdType.MESH
 f32 = jnp.float32
@@ -127,7 +127,7 @@
 
     @pl.when(chip == 0)
     def _():
-        spread(queries, range(1, RING))
+        spread(queries, (1, 2, 3, 6, 7, 4, 5))
 
 
     dkacc[...] = jnp.zeros_like(dkacc)

time: 79 us -> 78.7 us (level)
  no operation moved by 1% of the time
where the time goes in v4:
time: 78.7 us; the launch traced here: 78.5 us
  Pallas kernels  73.5 us (93%)
  local copies, waits for them, and re-layouts  4.38 us (6%)
    pallas_call x1, Pallas kernels, per_device(): pl.pallas_call(lambda *refs: kernel(rows, *refs), out_shape=(jax.ShapeDty...  73.5 us
    unnamed x7, local copies, waits for them, and re-layouts  4.38 us

profile of v4, /device:TPU:127, one launch (start us, length us, event | category | flops | bytes accessed | tf_op | source)
XLA Modules:
  0.0 78.5 jit_solution(7019209054816449691)
XLA Ops:
  0.6 73.5 %shard_map.67 = (f32[128,2048]{1,0:T(8,128)}, f32[128,1024]{1,0:T(8,128)}, f32[128,1024]{1,0:T(8,128)}) custom-call(f32[128,2048]{1,0:T(8,128)} %refs_0_.1, f32[128,1024]{1,0:T(8,128)} %refs_1_.1, f32[128,1024]{1,0:T(8,128)} %refs_2_.1, f32[128,2048]{1,0:T(8,128)} %refs_3_.1), custom_call_target="tpu_custom_call" | custom-call | flops 3355443200 | bytes 6291456 | tf_op jit(solution)/shard_map/pallas_call | solution.py:386
  74.1 0.0 copy-start.1
  74.1 2.4 %copy.10 = f32[128,2048]{1,0:T(8,128)} copy(f32[128,2048]{1,0:T(8,128)} %get-tuple-element.6) | data formatting | bytes 2097152
  76.5 0.0 copy-done.1
  76.5 0.0 copy-start
  76.5 0.8 %copy.11 = f32[128,1024]{1,0:T(8,128)} copy(f32[128,1024]{1,0:T(8,128)S(1)} %copy-done.1) | data formatting | bytes 1048576
  77.3 0.4 copy-done
  77.7 0.8 %copy.12 = f32[128,1024]{1,0:T(8,128)} copy(f32[128,1024]{1,0:T(8,128)S(1)} %copy-done) | data formatting | bytes 1048576
Async XLA Ops:
  74.1 2.4 %copy-start.1 = (f32[128,1024]{1,0:T(8,128)S(1)}, f32[128,1024]{1,0:T(8,128)}, u32[]{:S(2)}) copy-start(f32[128,1024]{1,0:T(8,128)} %get-tuple-element.7) | copy-start | bytes 1572868
  76.5 1.2 %copy-start = (f32[128,1024]{1,0:T(8,128)S(1)}, f32[128,1024]{1,0:T(8,128)}, u32[]{:S(2)}) copy-start(f32[128,1024]{1,0:T(8,128)} %get-tuple-element.8) | copy-start | bytes 1572868
